TPU v7x, 512 devices: a whole 4x4x16 slice. The times are simulated.
512 devices in a mesh: row: 32 (over z, core), col: 16 (over y, x).
Axes of the slice: x: 4, y: 4, z: 16, core: 2. Of those that a mesh axis runs over, the one named last changes fastest.
Arguments:
- flow_tiles: bfloat16 [32, 32, 256, 256], P('row', 'col'), may hold values from 0.1 to 25
- tile_cols: int32 [32, 32], P('row', 'col'), may hold values from -1 to 31, as said below
- pairs: int32 [32768, 2], P(('row', 'col')), may hold values from -1 to 31, as said below
Outputs:
- new_flow: float32 [32, 32, 256, 256], P('row', 'col')
Inputs may be any that keep to these rules, and one draw needn't show every extreme that they name: `tile_cols`: the stored slots of device (r, c) have distinct tile columns, each congruent to c modulo the col axis's size; tile row r stores tile column r. `pairs`: device (r, c) lists, in some order and without repeats, exactly the (k, s) for which slot s of the device is stored and M[r, k] and M[k, tile_cols[r, c * 2 + s]] are both stored tiles; its other rows are (-1, -1). Some device uses all 64 rows.
All inputs are finite; a program needn't handle non-finite values.
Results may differ from a plain program's by a relative error of at most 0.0003.
Values may be sent and summed in bfloat16 or wider, within the bound.
No kernel may reach another device: no remote copies, remote signals or barrier semaphores. Data moves between devices by JAX's collectives and lax.ppermute only.
A program may use at most 64 MiB of HBM per device.

v0:
```python
import jax
import jax.numpy as jnp
from jax import lax
from jax.sharding import PartitionSpec as P


def copy_for_each(shard, axis):
    length = lax.axis_size(axis)
    return lax.all_to_all(
        jnp.broadcast_to(shard[None], (length, *shard.shape)), axis, 0, 0, tiled=True
    )


def over_copies(shard, axis):
    return copy_for_each(shard, axis).sum(axis=0)


def block_products(
    initial, left_source, right_source, left_index, right_row, right_slot, weight, groups
):
    tile_count = weight.shape[1]
    left_index = left_index.reshape(groups, -1)
    right_row = right_row.reshape(groups, -1)
    right_slot = right_slot.reshape(groups, -1)
    weight = weight.reshape(groups, -1, tile_count)

    def block_step(carried, inputs):
        left_pick, row_pick, slot_pick, weight_block = inputs
        left_tiles = left_source[left_pick]
        right_tiles = right_source[row_pick, slot_pick]
        products = jnp.einsum(
            "pab,pbc->pac", left_tiles, right_tiles, preferred_element_type=jnp.float32
        )
        added = jnp.einsum("ps,pac->sac", weight_block, products, precision=lax.Precision.HIGHEST)
        return (carried + added, None)

    result, unused = lax.scan(block_step, initial, (left_index, right_row, right_slot, weight))
    return result


def on_device(flow_tiles, tile_cols, pairs):
    tile_count = flow_tiles.shape[1]
    tile_width = flow_tiles.shape[3]
    col_count = lax.axis_size("col")
    rows_total = lax.axis_size("row") * tile_width
    col_index = lax.axis_index("col")
    row_tiles, row_cols = (
        lax.all_gather(flow_tiles, "col", axis=1, tiled=True),
        lax.all_gather(tile_cols, "col", axis=1, tiled=True),
    )
    own_cols = tile_cols[0]
    inner_tile = pairs[:, 0]
    slot_list = pairs[:, 1]
    is_live = inner_tile >= 0
    inner_safe = jnp.maximum(inner_tile, 0)
    slot_safe = jnp.maximum(slot_list, 0)
    wanted = own_cols[slot_safe]
    left_index = jnp.argmax(row_cols[0][None, :] == inner_safe[:, None], axis=1)
    slot_ids = jnp.arange(tile_count, dtype=jnp.int32)
    weight = (is_live[:, None] & (slot_list[:, None] == slot_ids[None, :])).astype(jnp.float32)
    initial = jnp.zeros((tile_count, tile_width, tile_width), jnp.float32)
    column_tiles, column_cols = (
        lax.all_gather(flow_tiles, "row", axis=0, tiled=True),
        lax.all_gather(tile_cols, "row", axis=0, tiled=True),
    )
    right_slot = jnp.argmax(column_cols[inner_safe] == wanted[:, None], axis=1)
    expanded = block_products(
        initial, row_tiles[0], column_tiles, left_index, inner_safe, right_slot, weight, 4
    )
    inflated = expanded * expanded
    partial_sums = jnp.sum(inflated, axis=1)
    targets = col_index + col_count * slot_ids
    matches = own_cols[None, :] == targets[:, None]
    canonical = jnp.sum(jnp.where(matches[:, :, None], partial_sums[None, :, :], 0.0), axis=1)
    totals = over_copies(canonical, "row")
    per_slot = jnp.sum(jnp.where(matches[:, :, None], totals[:, None, :], 0.0), axis=0)
    stored = own_cols >= 0
    per_slot = jnp.where(stored[:, None], per_slot, 1.0)
    normed = inflated * jnp.float32(rows_total) / per_slot[:, None, :]
    blended = 0.5 * flow_tiles[0].astype(jnp.float32) + 0.5 * normed
    blended = jnp.where(stored[:, None, None], blended, 0.0)
    return blended[None]


def solution(mesh):
    placed = (P("row", "col", None, None), P("row", "col"), P(("row", "col"), None))
    return jax.shard_map(
        on_device,
        mesh=mesh,
        in_specs=placed,
        out_specs=P("row", "col", None, None),
        check_vma=False,
    )
```

profile of v0, /device:TPU:2, one launch (start us, length us, event | category | flops | bytes accessed | tf_op | source)
XLA Modules:
  0.0 273.3 jit_solution(3193878392183024058)
XLA Ops:
  8.0 36.2 %all-gather = s32[32,1,2]{2,1,0:T(1,128)S(1)} all-gather(s32[1,1,2]{2,1,0:T(1,128)} %bitcast.62), channel_id=1, replica_groups=mesh['row'=32,'col'=16] {'row'}, dimensions={0}, use_global_device_ids=true | all-gather | bytes 264 | tf_op jit(solution)/shard_map/all_gather | solution.py:64
  45.6 2.0 maximum_reduce_fusion
  51.6 15.7 %all-reduce = s32[32]{0:T(128)S(1)} all-reduce(s32[32]{0:T(128)S(1)} %bitcast_dynamic-update-slice_fusion), channel_id=1, replica_groups=mesh['row'=32,'col'=16] {'col'}, use_global_device_ids=true, to_apply=%add | all-reduce | flops 32 | bytes 256
  69.8 11.9 %all-gather.4.cloned.1.call-done = bf16[1,32,256,256]{3,2,0,1:T(8,128)(2,1)} async-done(((bf16[1,2,256,256]{3,2,0,1:T(8,128)(2,1)}), bf16[1,32,256,256]{3,2,0,1:T(8,128)(2,1)}) %all-gather.4.cloned.1.call-update) | async-done | bytes 4194320 | tf_op jit(solution)/shard_map/all_gather | solution.py:48
  81.7 81.5 %all-gather.6.cloned.1.call-done = bf16[32,2,256,256]{3,2,1,0:T(8,128)(2,1)} async-done(((bf16[1,2,256,256]{3,2,1,0:T(8,128)(2,1)}), bf16[32,2,256,256]{3,2,1,0:T(8,128)(2,1)}) %all-gather.6.cloned.1.call-update) | async-done | bytes 8388624 | tf_op jit(solution)/shard_map/all_gather | solution.py:63
  163.2 79.1 %while.11 = (s32[]{:T(128)}, f32[2,256,256]{2,0,1:T(2,128)S(1)}, f32[4,16,2]{1,2,0:T(2,128)S(1)}, s32[4,16]{1,0:T(4,128)S(1)}, bf16[32,256,256]{2,1,0:T(8,128)(2...) while((s32[]{:T(128)}, f32[2,256,256]{2,0,1:T(2,128)S(1)}, ...), condition=%wide.region_3.4_spmd.clone, body=%wide.region_2.3_spmd.clone.sunk | while | flops 562300160 | bytes 22025908 | solution.py:37
  163.2 2.9 %gather_fusion = bf16[16,256,256]{2,1,0:T(8,128)(2,1)S(1)} fusion(bf16[32,256,256]{2,1,0:T(8,128)(2,1)} %get-tuple-element.180, s32[1024]{0:T(1024)S(1)} %pad_clamp_fusion.3), kind=kCustom, calls=%fused_computation.clone.clone.1 | custom fusion | bytes 4194368 | tf_op jit(solution)/shard_map/while/body/eval_jaxpr/gather | solution.py:29
  166.2 5.4 %gather_fusion.1 = bf16[16,256,256]{2,1,0:T(8,128)(2,1)} fusion(bf16[32,2,256,256]{3,2,1,0:T(8,128)(2,1)} %get-tuple-element.183, s32[16]{0:T(128)S(1)} %get-tuple-element.155), kind=kCustom, calls=%fused_computation.1.clone.clone.1 | custom fusion | bytes 4194432 | tf_op jit(solution)/shard_map/while/body/eval_jaxpr/gather | solution.py:30
  171.6 4.3 %fusion.31 = f32[16,256,256]{2,1,0:T(8,128)} fusion(bf16[16,256,256]{2,1,0:T(8,128)(2,1)S(1)} %gather_fusion, bf16[16,256,256]{2,1,0:T(8,128)(2,1)} %gather_fusion.1), kind=kOutput, calls=%fused_computation.45.clone.1 | convolution fusion | flops 536870912 | bytes 8388608 | tf_op jit(solution)/shard_map/while/body/eval_jaxpr/pab,pbc->pac/dot_general | solution.py:31
  175.8 7.2 %fusion.32 = f32[2,256,256]{2,0,1:T(2,128)S(1)} fusion(f32[16,256,256]{2,1,0:T(8,128)} %fusion.31, f32[2,256,256]{2,0,1:T(2,128)S(1)} %get-tuple-element.167, pred[]{:T(512)S(6)} %compare.10, f32[4,16,2]{1,2,0:T(2,128)S(1)} %get-tuple-element.178, s32[]{:T(128)} %get-tuple-element.166), kind=kOutput, calls=%fused_computation.5.clone.1 | convolution fusion | flops 25427968 | bytes 5243909 | tf_op jit(solution)/shard_map/while/body/eval_jaxpr/ps,pac->sac/dot_general | solution.py:34
  183.1 2.9 %gather_fusion = bf16[16,256,256]{2,1,0:T(8,128)(2,1)S(1)} fusion(bf16[32,256,256]{2,1,0:T(8,128)(2,1)} %get-tuple-element.180, s32[1024]{0:T(1024)S(1)} %pad_clamp_fusion.3), kind=kCustom, calls=%fused_computation.clone.clone.1 | custom fusion | bytes 4194368 | tf_op jit(solution)/shard_map/while/body/eval_jaxpr/gather | solution.py:29
  185.9 5.4 %gather_fusion.1 = bf16[16,256,256]{2,1,0:T(8,128)(2,1)} fusion(bf16[32,2,256,256]{3,2,1,0:T(8,128)(2,1)} %get-tuple-element.183, s32[16]{0:T(128)S(1)} %get-tuple-element.155), kind=kCustom, calls=%fused_computation.1.clone.clone.1 | custom fusion | bytes 4194432 | tf_op jit(solution)/shard_map/while/body/eval_jaxpr/gather | solution.py:30
  191.3 4.3 %fusion.31 = f32[16,256,256]{2,1,0:T(8,128)} fusion(bf16[16,256,256]{2,1,0:T(8,128)(2,1)S(1)} %gather_fusion, bf16[16,256,256]{2,1,0:T(8,128)(2,1)} %gather_fusion.1), kind=kOutput, calls=%fused_computation.45.clone.1 | convolution fusion | flops 536870912 | bytes 8388608 | tf_op jit(solution)/shard_map/while/body/eval_jaxpr/pab,pbc->pac/dot_general | solution.py:31
  195.6 7.2 %fusion.32 = f32[2,256,256]{2,0,1:T(2,128)S(1)} fusion(f32[16,256,256]{2,1,0:T(8,128)} %fusion.31, f32[2,256,256]{2,0,1:T(2,128)S(1)} %get-tuple-element.167, pred[]{:T(512)S(6)} %compare.10, f32[4,16,2]{1,2,0:T(2,128)S(1)} %get-tuple-element.178, s32[]{:T(128)} %get-tuple-element.166), kind=kOutput, calls=%fused_computation.5.clone.1 | convolution fusion | flops 25427968 | bytes 5243909 | tf_op jit(solution)/shard_map/while/body/eval_jaxpr/ps,pac->sac/dot_general | solution.py:34
  202.8 2.9 %gather_fusion = bf16[16,256,256]{2,1,0:T(8,128)(2,1)S(1)} fusion(bf16[32,256,256]{2,1,0:T(8,128)(2,1)} %get-tuple-element.180, s32[1024]{0:T(1024)S(1)} %pad_clamp_fusion.3), kind=kCustom, calls=%fused_computation.clone.clone.1 | custom fusion | bytes 4194368 | tf_op jit(solution)/shard_map/while/body/eval_jaxpr/gather | solution.py:29
  205.7 5.4 %gather_fusion.1 = bf16[16,256,256]{2,1,0:T(8,128)(2,1)} fusion(bf16[32,2,256,256]{3,2,1,0:T(8,128)(2,1)} %get-tuple-element.183, s32[16]{0:T(128)S(1)} %get-tuple-element.155), kind=kCustom, calls=%fused_computation.1.clone.clone.1 | custom fusion | bytes 4194432 | tf_op jit(solution)/shard_map/while/body/eval_jaxpr/gather | solution.py:30
  211.1 4.3 %fusion.31 = f32[16,256,256]{2,1,0:T(8,128)} fusion(bf16[16,256,256]{2,1,0:T(8,128)(2,1)S(1)} %gather_fusion, bf16[16,256,256]{2,1,0:T(8,128)(2,1)} %gather_fusion.1), kind=kOutput, calls=%fused_computation.45.clone.1 | convolution fusion | flops 536870912 | bytes 8388608 | tf_op jit(solution)/shard_map/while/body/eval_jaxpr/pab,pbc->pac/dot_general | solution.py:31
  215.4 7.2 %fusion.32 = f32[2,256,256]{2,0,1:T(2,128)S(1)} fusion(f32[16,256,256]{2,1,0:T(8,128)} %fusion.31, f32[2,256,256]{2,0,1:T(2,128)S(1)} %get-tuple-element.167, pred[]{:T(512)S(6)} %compare.10, f32[4,16,2]{1,2,0:T(2,128)S(1)} %get-tuple-element.178, s32[]{:T(128)} %get-tuple-element.166), kind=kOutput, calls=%fused_computation.5.clone.1 | convolution fusion | flops 25427968 | bytes 5243909 | tf_op jit(solution)/shard_map/while/body/eval_jaxpr/ps,pac->sac/dot_general | solution.py:34
  222.6 2.9 %gather_fusion = bf16[16,256,256]{2,1,0:T(8,128)(2,1)S(1)} fusion(bf16[32,256,256]{2,1,0:T(8,128)(2,1)} %get-tuple-element.180, s32[1024]{0:T(1024)S(1)} %pad_clamp_fusion.3), kind=kCustom, calls=%fused_computation.clone.clone.1 | custom fusion | bytes 4194368 | tf_op jit(solution)/shard_map/while/body/eval_jaxpr/gather | solution.py:29
  225.5 5.4 %gather_fusion.1 = bf16[16,256,256]{2,1,0:T(8,128)(2,1)} fusion(bf16[32,2,256,256]{3,2,1,0:T(8,128)(2,1)} %get-tuple-element.183, s32[16]{0:T(128)S(1)} %get-tuple-element.155), kind=kCustom, calls=%fused_computation.1.clone.clone.1 | custom fusion | bytes 4194432 | tf_op jit(solution)/shard_map/while/body/eval_jaxpr/gather | solution.py:30
  230.9 4.3 %fusion.31 = f32[16,256,256]{2,1,0:T(8,128)} fusion(bf16[16,256,256]{2,1,0:T(8,128)(2,1)S(1)} %gather_fusion, bf16[16,256,256]{2,1,0:T(8,128)(2,1)} %gather_fusion.1), kind=kOutput, calls=%fused_computation.45.clone.1 | convolution fusion | flops 536870912 | bytes 8388608 | tf_op jit(solution)/shard_map/while/body/eval_jaxpr/pab,pbc->pac/dot_general | solution.py:31
  235.2 7.2 %fusion.32 = f32[2,256,256]{2,0,1:T(2,128)S(1)} fusion(f32[16,256,256]{2,1,0:T(8,128)} %fusion.31, f32[2,256,256]{2,0,1:T(2,128)S(1)} %get-tuple-element.167, pred[]{:T(512)S(6)} %compare.10, f32[4,16,2]{1,2,0:T(2,128)S(1)} %get-tuple-element.178, s32[]{:T(128)} %get-tuple-element.166), kind=kOutput, calls=%fused_computation.5.clone.1 | convolution fusion | flops 25427968 | bytes 5243909 | tf_op jit(solution)/shard_map/while/body/eval_jaxpr/ps,pac->sac/dot_general | solution.py:34
  243.2 7.8 %all-to-all-start = ((f32[32,2,256]{2,1,0:T(2,128)}), f32[32,2,256]{2,1,0:T(2,128)S(1)}, u32[]{:S(2)}, u32[]{:S(2)}) async-start(f32[32,2,256]{2,1,0:T(2,128)} %broadcast_in_dim.93), calls=%async_computation | async-start | bytes 131072 | tf_op jit(solution)/shard_map/all_to_all | solution.py:9
  250.9 14.4 %all-to-all-done = f32[32,2,256]{2,1,0:T(2,128)S(1)} async-done(((f32[32,2,256]{2,1,0:T(2,128)}), f32[32,2,256]{2,1,0:T(2,128)S(1)}, u32[]{:S(2)}, u32[]{:S(2)}) %all-to-all-start) | async-done | bytes 65568 | tf_op jit(solution)/shard_map/all_to_all | solution.py:9
  (42 shorter events, 10.6 us)
Async XLA Ops:
  6.5 75.2 %all-gather.4.cloned.1.call-start = ((), (), s32[]{:S(2)}) async-start(), calls=%async_computation.1 | async-start | bytes 4456448 | tf_op jit(solution)/shard_map/all_gather | solution.py:48
  7.3 156.0 %all-gather.6.cloned.1.call-start = ((), (), s32[]{:S(2)}) async-start(), calls=%async_computation.2 | async-start | bytes 8650752 | tf_op jit(solution)/shard_map/all_gather | solution.py:63
  163.2 87.7 %copy-start.1 = (s32[1,2]{1,0:T(1,128)S(1)}, s32[1,2]{1,0:T(1,128)}, u32[]{:S(2)}) copy-start(s32[1,2]{1,0:T(1,128)} %param.6) | copy-start | bytes 28
  163.2 102.3 %copy-start = (bf16[1,2,256,256]{3,2,1,0:T(8,128)(2,1)S(1)}, bf16[1,2,256,256]{3,2,1,0:T(8,128)(2,1)}, u32[]{:S(2)}) copy-start(bf16[1,2,256,256]{3,2,1,0:T(8,128)(2,1)} %param.5) | copy-start | bytes 786436
  243.2 22.2 %all-to-all-start = ((f32[32,2,256]{2,1,0:T(2,128)}), f32[32,2,256]{2,1,0:T(2,128)S(1)}, u32[]{:S(2)}, u32[]{:S(2)}) async-start(f32[32,2,256]{2,1,0:T(2,128)} %broadcast_in_dim.93), calls=%async_computation | async-start | bytes 131072 | tf_op jit(solution)/shard_map/all_to_all | solution.py:9
Sparse Core Ops, SparseCore 0:
  10.4 71.3 all-gather.3
  83.9 79.2 all-gather.5
where the time goes:
time: 274 us; the launch traced here: 273 us
  waiting for transfers between devices  109 us (40%)
  blocking collectives  52 us (19%)
  matrix products  45.8 us (17%)
  local copies, waits for them, and re-layouts  38.2 us (14%)
  between operations  14.1 us (5%)
  starting transfers between devices  7.8 us (3%)
  other arithmetic  6.17 us (2%)
    all_gather x1, waiting for transfers between devices, on_device(): lax.all_gather(flow_tiles, 'row', axis=0, tiled=True)  81.5 us
    all_gather x1, blocking collectives, on_device(): lax.all_gather(tile_cols, 'row', axis=0, tiled=True)  36.2 us
    dot_general x4, matrix products, block_step(): jnp.einsum('ps,pac->sac', weight_block, products, precision=lax.Precision...  28.7 us
    gather x4, local copies, waits for them, and re-layouts, block_step(): right_tiles = right_source[row_pick, slot_pick]  21.7 us
    dot_general x4, matrix products, block_step(): jnp.einsum('pab,pbc->pac', left_tiles, right_tiles, preferred_element_typ...  17 us
    unnamed x1, blocking collectives  15.7 us
    all_to_all x1, waiting for transfers between devices, copy_for_each(): lax.all_to_all(jnp.broadcast_to(shard[None], (length, *shard.shape)), axi...  14.4 us
    all_gather x1, waiting for transfers between devices, on_device(): lax.all_gather(flow_tiles, 'col', axis=1, tiled=True)  11.9 us
  transfers between devices with their start and end apart: 3, of which 3 were waited for; matrix products, arithmetic and copies ran while one was open for 3% of the time, Pallas kernels for 0%

commit v1 on v0

--- a/solution.py
+++ b/solution.py
@@ -2,6 +2,7 @@
 import jax.numpy as jnp
 from jax import lax
 from jax.sharding import PartitionSpec as P
+from jax.lax import all_to_all, psum
 
 
 def copy_for_each(shard, axis):
@@ -44,8 +45,15 @@
     col_count = lax.axis_size("col")
     rows_total = lax.axis_size("row") * tile_width
     col_index = lax.axis_index("col")
+
+    def choose_packet(x_local, dim_at):
+        reply = psum(1, axis_name="col")
+        seen_now = jnp.stack(reply * [x_local], axis=0)
+        e_next = all_to_all(seen_now, concat_axis=0, axis_name="col", split_axis=0)
+        return jnp.concatenate(e_next, axis=dim_at)
+
     row_tiles, row_cols = (
-        lax.all_gather(flow_tiles, "col", axis=1, tiled=True),
+        choose_packet(flow_tiles, 1),
         lax.all_gather(tile_cols, "col", axis=1, tiled=True),
     )
     own_cols = tile_cols[0]

time: 274 us -> 208 us (0.76)
  waiting for transfers between devices: 109 us -> 25.2 us
  starting transfers between devices: 7.8 us -> 21.5 us
  blocking collectives: 52 us -> 55.9 us
    all_gather x1, waiting for transfers between devices: 81.5 us -> 10.1 us  [on_device(): lax.all_gather(flow_tiles, 'row', axis=0, tiled=True)]
    all_gather x1 -> x0, waiting for transfers between devices: 11.9 us -> none  [on_device(): lax.all_gather(flow_tiles, 'col', axis=1, tiled=True)]
    all_to_all x0 -> x1, starting transfers between devices: none -> 10.3 us  [choose_packet(): e_next = all_to_all(seen_now, concat_axis=0, axis_name='col', split_axis=0)]
    unnamed x1, blocking collectives: 15.7 us -> 22.6 us
    all_to_all x1, starting transfers between devices: 7.75 us -> 11.2 us  [copy_for_each(): lax.all_to_all(jnp.broadcast_to(shard[None], (length, *shard.shape)), axi...]
    another operation x0 -> x1, local copies, waits for them, and re-layouts: none -> 3.38 us  [choose_packet(): seen_now = jnp.stack(reply * [x_local], axis=0)]
    all_gather x1, blocking collectives: 36.2 us -> 33.4 us  [on_device(): lax.all_gather(tile_cols, 'row', axis=0, tiled=True)]
  transfers between devices with their start and end apart: 3 -> 3, of which waited for: 3 -> 2; matrix products, arithmetic and copies ran while one was open for 3% -> 4% of each run, Pallas kernels for 0% -> 0%
where the time goes in v1:
time: 208 us; the launch traced here: 207 us
  blocking collectives  55.9 us (27%)
  matrix products  45.8 us (22%)
  local copies, waits for them, and re-layouts  40.2 us (19%)
  waiting for transfers between devices  25.2 us (12%)
  starting transfers between devices  21.5 us (10%)
  between operations  14 us (7%)
  other arithmetic  4.01 us (2%)
    all_gather x1, blocking collectives, on_device(): lax.all_gather(tile_cols, 'row', axis=0, tiled=True)  33.4 us
    dot_general x4, matrix products, block_step(): jnp.einsum('ps,pac->sac', weight_block, products, precision=lax.Precision...  28.7 us
    unnamed x1, blocking collectives  22.6 us
    gather x4, local copies, waits for them, and re-layouts, block_step(): right_tiles = right_source[row_pick, slot_pick]  21.7 us
    dot_general x4, matrix products, block_step(): jnp.einsum('pab,pbc->pac', left_tiles, right_tiles, preferred_element_typ...  17 us
    all_to_all x1, waiting for transfers between devices, copy_for_each(): lax.all_to_all(jnp.broadcast_to(shard[None], (length, *shard.shape)), axi...  14.4 us
    gather x4, local copies, waits for them, and re-layouts, block_step(): left_tiles = left_source[left_pick]  11.5 us
    all_to_all x1, starting transfers between devices, copy_for_each(): lax.all_to_all(jnp.broadcast_to(shard[None], (length, *shard.shape)), axi...  11.2 us
  transfers between devices with their start and end apart: 3, of which 2 were waited for; matrix products, arithmetic and copies ran while one was open for 4% of the time, Pallas kernels for 0%

profile of v1, /device:TPU:2, one launch (start us, length us, event | category | flops | bytes accessed | tf_op | source)
XLA Modules:
  0.0 206.8 jit_solution(8213955774099644570)
XLA Ops:
  7.3 3.4 %stack.2 = bf16[16,1,2,256,256]{4,3,2,1,0:T(8,128)(2,1)} broadcast(bf16[2,256,256]{2,1,0:T(8,128)(2,1)} %bitcast.58), dimensions={2,3,4} | broadcast | bytes 4456448 | tf_op jit(solution)/shard_map/stack | solution.py:51
  10.6 10.3 %all-to-all-start = ((bf16[16,1,2,256,256]{4,3,2,1,0:T(8,128)(2,1)}), bf16[16,1,2,256,256]{4,3,2,1,0:T(8,128)(2,1)}, u32[]{:S(2)}, u32[]{:S(2)}) async-start(bf16[16,1,2,256,256]{4,3,2,1,0:T(8,128)(2,1)} %stack.2), calls=%async_computation | async-start | bytes 8388608 | tf_op jit(solution)/shard_map/all_to_all | solution.py:52
  21.0 33.4 %all-gather = s32[32,1,2]{2,1,0:T(1,128)S(1)} all-gather(s32[1,1,2]{2,1,0:T(1,128)S(1)} %bitcast.59), channel_id=1, replica_groups=mesh['row'=32,'col'=16] {'row'}, dimensions={0}, use_global_device_ids=true | all-gather | bytes 264 | tf_op jit(solution)/shard_map/all_gather | solution.py:72
  59.5 22.6 %all-reduce = s32[32]{0:T(128)S(1)} all-reduce(s32[32]{0:T(128)S(1)} %bitcast_dynamic-update-slice_fusion), channel_id=1, replica_groups=mesh['row'=32,'col'=16] {'col'}, use_global_device_ids=true, to_apply=%add | all-reduce | flops 32 | bytes 256
  83.1 10.1 %all-gather.3.cloned.1.call-done = bf16[32,2,256,256]{3,2,1,0:T(8,128)(2,1)} async-done(((bf16[1,2,256,256]{3,2,1,0:T(8,128)(2,1)}), bf16[32,2,256,256]{3,2,1,0:T(8,128)(2,1)}) %all-gather.3.cloned.1.call-update) | async-done | bytes 8388624 | tf_op jit(solution)/shard_map/all_gather | solution.py:71
  93.2 79.1 %while.11 = (s32[]{:T(128)}, f32[2,256,256]{2,0,1:T(2,128)S(1)}, f32[4,16,2]{1,2,0:T(2,128)S(1)}, s32[4,16]{1,0:T(4,128)S(1)}, bf16[32,256,256]{2,1,0:T(8,128)(2...) while((s32[]{:T(128)}, f32[2,256,256]{2,0,1:T(2,128)S(1)}, ...), condition=%wide.region_3.4_spmd.clone, body=%wide.region_2.3_spmd.clone.sunk | while | flops 562300160 | bytes 22025908 | solution.py:38
  93.3 2.9 %gather_fusion = bf16[16,256,256]{2,1,0:T(8,128)(2,1)S(1)} fusion(bf16[32,256,256]{2,1,0:T(8,128)(2,1)} %get-tuple-element.180, s32[1024]{0:T(1024)S(1)} %pad_clamp_fusion.3), kind=kCustom, calls=%fused_computation.clone.clone.1 | custom fusion | bytes 4194368 | tf_op jit(solution)/shard_map/while/body/eval_jaxpr/gather | solution.py:30
  96.2 5.4 %gather_fusion.1 = bf16[16,256,256]{2,1,0:T(8,128)(2,1)} fusion(bf16[32,2,256,256]{3,2,1,0:T(8,128)(2,1)} %get-tuple-element.183, s32[16]{0:T(128)S(1)} %get-tuple-element.155), kind=kCustom, calls=%fused_computation.1.clone.clone.1 | custom fusion | bytes 4194432 | tf_op jit(solution)/shard_map/while/body/eval_jaxpr/gather | solution.py:31
  101.6 4.3 %fusion.28 = f32[16,256,256]{2,1,0:T(8,128)} fusion(bf16[16,256,256]{2,1,0:T(8,128)(2,1)S(1)} %gather_fusion, bf16[16,256,256]{2,1,0:T(8,128)(2,1)} %gather_fusion.1), kind=kOutput, calls=%fused_computation.42.clone.1 | convolution fusion | flops 536870912 | bytes 8388608 | tf_op jit(solution)/shard_map/while/body/eval_jaxpr/pab,pbc->pac/dot_general | solution.py:32
  105.9 7.2 %fusion.29 = f32[2,256,256]{2,0,1:T(2,128)S(1)} fusion(f32[16,256,256]{2,1,0:T(8,128)} %fusion.28, f32[2,256,256]{2,0,1:T(2,128)S(1)} %get-tuple-element.167, pred[]{:T(512)S(6)} %compare.10, f32[4,16,2]{1,2,0:T(2,128)S(1)} %get-tuple-element.178, s32[]{:T(128)} %get-tuple-element.166), kind=kOutput, calls=%fused_computation.5.clone.1 | convolution fusion | flops 25427968 | bytes 5243909 | tf_op jit(solution)/shard_map/while/body/eval_jaxpr/ps,pac->sac/dot_general | solution.py:35
  113.1 2.9 %gather_fusion = bf16[16,256,256]{2,1,0:T(8,128)(2,1)S(1)} fusion(bf16[32,256,256]{2,1,0:T(8,128)(2,1)} %get-tuple-element.180, s32[1024]{0:T(1024)S(1)} %pad_clamp_fusion.3), kind=kCustom, calls=%fused_computation.clone.clone.1 | custom fusion | bytes 4194368 | tf_op jit(solution)/shard_map/while/body/eval_jaxpr/gather | solution.py:30
  116.0 5.4 %gather_fusion.1 = bf16[16,256,256]{2,1,0:T(8,128)(2,1)} fusion(bf16[32,2,256,256]{3,2,1,0:T(8,128)(2,1)} %get-tuple-element.183, s32[16]{0:T(128)S(1)} %get-tuple-element.155), kind=kCustom, calls=%fused_computation.1.clone.clone.1 | custom fusion | bytes 4194432 | tf_op jit(solution)/shard_map/while/body/eval_jaxpr/gather | solution.py:31
  121.4 4.3 %fusion.28 = f32[16,256,256]{2,1,0:T(8,128)} fusion(bf16[16,256,256]{2,1,0:T(8,128)(2,1)S(1)} %gather_fusion, bf16[16,256,256]{2,1,0:T(8,128)(2,1)} %gather_fusion.1), kind=kOutput, calls=%fused_computation.42.clone.1 | convolution fusion | flops 536870912 | bytes 8388608 | tf_op jit(solution)/shard_map/while/body/eval_jaxpr/pab,pbc->pac/dot_general | solution.py:32
  125.6 7.2 %fusion.29 = f32[2,256,256]{2,0,1:T(2,128)S(1)} fusion(f32[16,256,256]{2,1,0:T(8,128)} %fusion.28, f32[2,256,256]{2,0,1:T(2,128)S(1)} %get-tuple-element.167, pred[]{:T(512)S(6)} %compare.10, f32[4,16,2]{1,2,0:T(2,128)S(1)} %get-tuple-element.178, s32[]{:T(128)} %get-tuple-element.166), kind=kOutput, calls=%fused_computation.5.clone.1 | convolution fusion | flops 25427968 | bytes 5243909 | tf_op jit(solution)/shard_map/while/body/eval_jaxpr/ps,pac->sac/dot_general | solution.py:35
  132.9 2.9 %gather_fusion = bf16[16,256,256]{2,1,0:T(8,128)(2,1)S(1)} fusion(bf16[32,256,256]{2,1,0:T(8,128)(2,1)} %get-tuple-element.180, s32[1024]{0:T(1024)S(1)} %pad_clamp_fusion.3), kind=kCustom, calls=%fused_computation.clone.clone.1 | custom fusion | bytes 4194368 | tf_op jit(solution)/shard_map/while/body/eval_jaxpr/gather | solution.py:30
  135.7 5.4 %gather_fusion.1 = bf16[16,256,256]{2,1,0:T(8,128)(2,1)} fusion(bf16[32,2,256,256]{3,2,1,0:T(8,128)(2,1)} %get-tuple-element.183, s32[16]{0:T(128)S(1)} %get-tuple-element.155), kind=kCustom, calls=%fused_computation.1.clone.clone.1 | custom fusion | bytes 4194432 | tf_op jit(solution)/shard_map/while/body/eval_jaxpr/gather | solution.py:31
  141.2 4.3 %fusion.28 = f32[16,256,256]{2,1,0:T(8,128)} fusion(bf16[16,256,256]{2,1,0:T(8,128)(2,1)S(1)} %gather_fusion, bf16[16,256,256]{2,1,0:T(8,128)(2,1)} %gather_fusion.1), kind=kOutput, calls=%fused_computation.42.clone.1 | convolution fusion | flops 536870912 | bytes 8388608 | tf_op jit(solution)/shard_map/while/body/eval_jaxpr/pab,pbc->pac/dot_general | solution.py:32
  145.4 7.2 %fusion.29 = f32[2,256,256]{2,0,1:T(2,128)S(1)} fusion(f32[16,256,256]{2,1,0:T(8,128)} %fusion.28, f32[2,256,256]{2,0,1:T(2,128)S(1)} %get-tuple-element.167, pred[]{:T(512)S(6)} %compare.10, f32[4,16,2]{1,2,0:T(2,128)S(1)} %get-tuple-element.178, s32[]{:T(128)} %get-tuple-element.166), kind=kOutput, calls=%fused_computation.5.clone.1 | convolution fusion | flops 25427968 | bytes 5243909 | tf_op jit(solution)/shard_map/while/body/eval_jaxpr/ps,pac->sac/dot_general | solution.py:35
  152.7 2.9 %gather_fusion = bf16[16,256,256]{2,1,0:T(8,128)(2,1)S(1)} fusion(bf16[32,256,256]{2,1,0:T(8,128)(2,1)} %get-tuple-element.180, s32[1024]{0:T(1024)S(1)} %pad_clamp_fusion.3), kind=kCustom, calls=%fused_computation.clone.clone.1 | custom fusion | bytes 4194368 | tf_op jit(solution)/shard_map/while/body/eval_jaxpr/gather | solution.py:30
  155.5 5.4 %gather_fusion.1 = bf16[16,256,256]{2,1,0:T(8,128)(2,1)} fusion(bf16[32,2,256,256]{3,2,1,0:T(8,128)(2,1)} %get-tuple-element.183, s32[16]{0:T(128)S(1)} %get-tuple-element.155), kind=kCustom, calls=%fused_computation.1.clone.clone.1 | custom fusion | bytes 4194432 | tf_op jit(solution)/shard_map/while/body/eval_jaxpr/gather | solution.py:31
  160.9 4.3 %fusion.28 = f32[16,256,256]{2,1,0:T(8,128)} fusion(bf16[16,256,256]{2,1,0:T(8,128)(2,1)S(1)} %gather_fusion, bf16[16,256,256]{2,1,0:T(8,128)(2,1)} %gather_fusion.1), kind=kOutput, calls=%fused_computation.42.clone.1 | convolution fusion | flops 536870912 | bytes 8388608 | tf_op jit(solution)/shard_map/while/body/eval_jaxpr/pab,pbc->pac/dot_general | solution.py:32
  165.2 7.2 %fusion.29 = f32[2,256,256]{2,0,1:T(2,128)S(1)} fusion(f32[16,256,256]{2,1,0:T(8,128)} %fusion.28, f32[2,256,256]{2,0,1:T(2,128)S(1)} %get-tuple-element.167, pred[]{:T(512)S(6)} %compare.10, f32[4,16,2]{1,2,0:T(2,128)S(1)} %get-tuple-element.178, s32[]{:T(128)} %get-tuple-element.166), kind=kOutput, calls=%fused_computation.5.clone.1 | convolution fusion | flops 25427968 | bytes 5243909 | tf_op jit(solution)/shard_map/while/body/eval_jaxpr/ps,pac->sac/dot_general | solution.py:35
  173.2 11.2 %all-to-all-start.1 = ((f32[32,2,256]{2,1,0:T(2,128)}), f32[32,2,256]{2,1,0:T(2,128)S(1)}, u32[]{:S(2)}, u32[]{:S(2)}) async-start(f32[32,2,256]{2,1,0:T(2,128)} %broadcast_in_dim.93), calls=%async_computation.1 | async-start | bytes 131072 | tf_op jit(solution)/shard_map/all_to_all | solution.py:10
  184.4 14.4 %all-to-all-done.1 = f32[32,2,256]{2,1,0:T(2,128)S(1)} async-done(((f32[32,2,256]{2,1,0:T(2,128)}), f32[32,2,256]{2,1,0:T(2,128)S(1)}, u32[]{:S(2)}, u32[]{:S(2)}) %all-to-all-start.1) | async-done | bytes 65568 | tf_op jit(solution)/shard_map/all_to_all | solution.py:10
  (44 shorter events, 8.4 us)
Async XLA Ops:
  6.5 86.7 %all-gather.3.cloned.1.call-start = ((), (), s32[]{:S(2)}) async-start(), calls=%async_computation.2 | async-start | bytes 8650752 | tf_op jit(solution)/shard_map/all_gather | solution.py:71
  10.6 10.3 %copy-start.1 = (s32[1,2]{1,0:T(1,128)S(1)}, s32[1,2]{1,0:T(1,128)}, u32[]{:S(2)}) copy-start(s32[1,2]{1,0:T(1,128)} %param.6) | copy-start | bytes 28
  10.6 44.3 %copy-start.2 = (s32[64,2]{0,1:T(2,128)S(1)}, s32[64,2]{0,1:T(2,128)}, u32[]{:S(2)}) copy-start(s32[64,2]{0,1:T(2,128)} %param.7) | copy-start | bytes 1540
  10.6 72.5 %all-to-all-start = ((bf16[16,1,2,256,256]{4,3,2,1,0:T(8,128)(2,1)}), bf16[16,1,2,256,256]{4,3,2,1,0:T(8,128)(2,1)}, u32[]{:S(2)}, u32[]{:S(2)}) async-start(bf16[16,1,2,256,256]{4,3,2,1,0:T(8,128)(2,1)} %stack.2), calls=%async_computation | async-start | bytes 8388608 | tf_op jit(solution)/shard_map/all_to_all | solution.py:52
  93.2 105.8 %copy-start = (bf16[1,2,256,256]{3,2,1,0:T(8,128)(2,1)S(1)}, bf16[1,2,256,256]{3,2,1,0:T(8,128)(2,1)}, u32[]{:S(2)}) copy-start(bf16[1,2,256,256]{3,2,1,0:T(8,128)(2,1)} %param.5) | copy-start | bytes 786436
  173.2 25.6 %all-to-all-start.1 = ((f32[32,2,256]{2,1,0:T(2,128)}), f32[32,2,256]{2,1,0:T(2,128)S(1)}, u32[]{:S(2)}, u32[]{:S(2)}) async-start(f32[32,2,256]{2,1,0:T(2,128)} %broadcast_in_dim.93), calls=%async_computation.1 | async-start | bytes 131072 | tf_op jit(solution)/shard_map/all_to_all | solution.py:10
Sparse Core Ops, SparseCore 0:
  9.5 83.7 all-gather.2
